TPU v7x, 128 devices: a whole 4x4x4 slice. The times are simulated.
128 devices in a mesh: comp: 2 (over core), dom: 64 (over z, y, x).
Axes of the slice: x: 4, y: 4, z: 4, core: 2. Of those that a mesh axis runs over, the one named last changes fastest.
Arguments:
- state: bfloat16 [4, 64, 131072], P(None, None, ('comp', 'dom')), may hold values from -6 to 6
- links: int32 [8, 131072], P(None, ('comp', 'dom')), may hold values from -512 to 512, as said below
- link_weight: float32 [8, 131072], P(None, ('comp', 'dom')), may hold values from 0 to 0.4, as said below
- point_mass: float32 [131072], P(('comp', 'dom')), may hold values from 2 to 8
- flow: float32 [2, 131072], P(None, ('comp', 'dom')), may hold values from -1 to 1
- ov_src: int32 [1048576], P(('comp', 'dom')), may hold values from 0 to 1023
- ov_owner: int32 [1048576, 1], P(('comp', 'dom')), may hold values from 0 to 63; in each aligned block of 8192 rows (0 to 8191, 8192 to 16383, ...) at most 512 rows name the same one
- ov_row: int32 [1048576], P(('comp', 'dom')), may hold values from 0 to 1023
- ov_weight: float32 [1048576], P(('comp', 'dom')), may hold values from 0.2 to 0.6
Outputs:
- new_state: bfloat16 [4, 64, 131072], P(None, None, ('comp', 'dom'))
- surface_import: float32 [4, 131072], P(None, ('comp', 'dom'))
Inputs may be any that keep to these rules, and one draw needn't show every extreme that they name: The first 1 to 3 slots (atmosphere) or 5 to 7 slots (ocean) of a column are real links; the remaining slots are 0. `link_weight`: zero exactly on the padding slots. `ov_owner`: within the 8192 entries of one device no owner is named more than 512 times, a bound that some block reaches.
All inputs are finite; a program needn't handle non-finite values.
Results may differ from a plain program's by a relative error of at most 0.0065.
Values may be sent and summed in bfloat16 or wider, within the bound.
A program may use at most 128 MiB of HBM per device.

v0:
```python
import functools
import math

import jax
import jax.numpy as jnp
import numpy as np
from jax import lax
from jax.experimental import pallas as pl
from jax.experimental.pallas import tpu as pltpu
from jax.sharding import PartitionSpec as P

CH = 4
LEV = 64
ROWS = 1024
HW = 512
BLK = 256
NB = ROWS // BLK
SPAN = BLK + 2 * HW
OWNERS = 64
ENT = 8192
SLAB = 1024
TAIL = 16
MESH = pl.DeviceIdType.MESH
BF = jnp.bfloat16
F32 = jnp.float32


def derivative():
    nodes = np.array([-1.0, -1.0 / math.sqrt(5.0), 1.0 / math.sqrt(5.0), 1.0])
    weights = np.ones(4)
    for column in range(4):
        for middle in range(4):
            if middle != column:
                weights[column] = weights[column] / (nodes[column] - nodes[middle])
    table = np.zeros((4, 4))
    for target in range(4):
        for column in range(4):
            if column != target:
                table[target, column] = weights[column] / weights[target] / (nodes[target] - nodes[column])
        table[target, target] = -np.sum(table[target])
    return table


def constants():
    d = derivative()
    along_x = np.kron(np.eye(4), d)
    along_y = np.kron(d, np.eye(4))
    kx = -0.04 * np.kron(np.eye(BLK // 16), along_x.T)
    ky = -0.04 * np.kron(np.eye(BLK // 16), along_y.T)
    kxy = np.stack([kx, ky])
    second = np.zeros((LEV, LEV))
    for l in range(LEV):
        if l + 1 < LEV:
            second[l, l + 1] += 1.0
            second[l, l] -= 1.0
        if l > 0:
            second[l, l - 1] += 1.0
            second[l, l] -= 1.0
    vert = np.kron(np.eye(CH), second)
    pick = np.zeros((TAIL, CH * LEV))
    place = np.zeros((CH, TAIL, TAIL))
    tvert = np.zeros((TAIL, TAIL))
    for lev in range(4):
        for ch in range(CH):
            r = lev * 4 + ch
            pick[r, ch * LEV + lev] = 1.0
            place[ch, lev, r] = 1.0
            for other in range(4):
                tvert[r, other * 4 + ch] = second[lev, other]
    return (
        jnp.asarray(kxy, BF),
        jnp.asarray(vert, BF),
        jnp.asarray(pick, BF),
        jnp.asarray(place.reshape(CH * TAIL, TAIL), BF),
        jnp.asarray(tvert, BF),
    )


def dot(a, b):
    return lax.dot_general(a, b, (((1,), (0,)), ((), ())), preferred_element_type=F32)


def dot_t(a, b):
    return lax.dot_general(a, b, (((1,), (1,)), ((), ())), preferred_element_type=F32)


def body(
    state_ref, links_ref, lw_ref, mass_ref, flow_ref, src_ref, owner_ref, row_ref, w_ref,
    kxy_ref, vert_ref, pick_ref, place_ref, tvert_ref,
    out_ref, imp_ref,
    ext1, ext2, tail1, tail2, mixm, badv, ab, table, keys, acc, send, recv, imps,
    halo_send, halo_recv, a2a_send, a2a_recv,
):
    comp = lax.axis_index("comp")
    me = lax.axis_index("dom")
    other = 1 - comp
    right = lax.rem(me + 1, OWNERS)
    left = lax.rem(me + OWNERS - 1, OWNERS)
    mid = slice(HW, HW + ROWS)

    barrier = pltpu.get_barrier_semaphore()

    def greet(r, carry):
        pl.semaphore_signal(
            barrier, inc=1, device_id=(other, lax.rem(me + r, OWNERS)), device_id_type=MESH
        )
        return carry

    for side in (left, right):
        pl.semaphore_signal(barrier, inc=1, device_id=(comp, side), device_id_type=MESH)
    lax.fori_loop(0, OWNERS, greet, 0)

    def halo(ext, number):
        copies = []
        for side, src, dst, k in (
            (right, slice(ROWS, ROWS + HW), slice(0, HW), 0),
            (left, slice(HW, 2 * HW), slice(HW + ROWS, 2 * HW + ROWS), 1),
        ):
            copies.append(
                pltpu.make_async_remote_copy(
                    src_ref=ext.at[:, src],
                    dst_ref=ext.at[:, dst],
                    send_sem=halo_send.at[number, k],
                    recv_sem=halo_recv.at[number, k],
                    device_id=(comp, side),
                    device_id_type=MESH,
                )
            )
        return copies

    def advance(x, j):
        return (x.astype(F32) + dot(x, badv[j])).astype(BF)

    mass = mass_ref[...]
    total = jnp.sum(lw_ref[...], axis=0, keepdims=True)

    @pl.when(comp == 0)
    def _():
        inv = 1.0 / (mass + total)
        ab[0:1, :] = mass * inv
        ab[1:2, :] = inv
        for j in range(NB):
            cols = slice(j * BLK, (j + 1) * BLK)
            badv[j] = (
                kxy_ref[0].astype(F32) * flow_ref[0:1, cols] + kxy_ref[1].astype(F32) * flow_ref[1:2, cols]
            ).astype(BF)
        for j in range(NB):
            cols = slice(j * BLK, (j + 1) * BLK)
            ext1[:, HW + j * BLK : HW + (j + 1) * BLK] = advance(state_ref[:, cols], j)

    @pl.when(comp == 1)
    def _():
        half = 0.5 / mass
        ab[0:1, :] = 1.0 - half * total
        ab[1:2, :] = half
        ab[2:3, :] = 0.25 * flow_ref[0:1, :] * flow_ref[0:1, :]
        ext1[:, mid] = state_ref[...]

    pl.semaphore_wait(barrier, OWNERS + 2)
    deep1 = halo(ext1, 0)
    for copy in deep1:
        copy.start()

    for ch in range(CH):
        line = state_ref[ch * LEV : ch * LEV + 1, :].astype(F32)
        for hi in range(8):
            table[ch * 8 + hi : ch * 8 + hi + 1, :] = line[:, hi * 128 : (hi + 1) * 128]
    source = src_ref[...]
    target = row_ref[...]
    relative = jnp.bitwise_and(owner_ref[...] - me + OWNERS, OWNERS - 1)
    first = relative * 8 + lax.shift_right_logical(target, 7)
    keys[0] = jnp.bitwise_and(source, 127).astype(F32)
    keys[1] = lax.shift_right_logical(source, 7).astype(F32)
    keys[2] = jnp.bitwise_and(target, 127).astype(F32)
    keys[3] = first.astype(F32)
    keys[4] = (first - 256).astype(F32)
    sub = lax.broadcasted_iota(jnp.int32, (8, 16, SLAB), 0) * 16 + lax.broadcasted_iota(jnp.int32, (8, 16, SLAB), 1)
    lanes = sub.astype(F32).astype(BF)
    upper = (sub + 128).astype(F32).astype(BF)
    high = lax.broadcasted_iota(jnp.int32, (8, SLAB), 0).astype(F32)
    exported = table[...].astype(BF)
    one, zero = jnp.asarray(1.0, BF), jnp.asarray(0.0, BF)
    chunks = SLAB // 128

    def row_of(which, i):
        return jnp.concatenate([keys[which, pl.ds(i * chunks + k, 1), :] for k in range(chunks)], axis=1)

    def wide(x):
        return jnp.broadcast_to(x, (16, SLAB)).astype(BF)[None]

    def remap(i, carry):
        hot = jnp.where(lanes == wide(row_of(0, i)), one, zero).reshape(128, SLAB)
        found = dot(exported, hot)
        chosen = high == row_of(1, i)
        weight = jnp.concatenate([w_ref[pl.ds(i * chunks + k, 1), :] for k in range(chunks)], axis=1)
        low = lanes == wide(row_of(2, i))
        rows = []
        for ch in range(CH):
            value = jnp.sum(jnp.where(chosen, found[ch * 8 : ch * 8 + 8], 0.0), axis=0, keepdims=True) * weight
            rows.append(jnp.where(low, wide(value), zero).reshape(128, SLAB))
        values = jnp.concatenate(rows, axis=0)
        ka, kb = wide(row_of(3, i)), wide(row_of(4, i))
        spots = jnp.concatenate(
            [
                jnp.where(part == key, one, zero).reshape(128, SLAB)
                for key in (ka, kb)
                for part in (lanes, upper)
            ],
            axis=0,
        )
        acc[...] += dot_t(spots, values)
        return carry

    acc[...] = jnp.zeros_like(acc)
    lax.fori_loop(0, ENT // SLAB, remap, 0)
    for pair in range(2):
        parts = [acc[:, c * 128 : (c + 1) * 128].reshape(OWNERS, 8, 128) for c in (2 * pair, 2 * pair + 1)]
        send[:, pair * 16 : pair * 16 + 16, :] = jnp.concatenate(parts, axis=1).astype(BF)

    def post(r, carry):
        pltpu.make_async_remote_copy(
            src_ref=send.at[r],
            dst_ref=recv.at[r],
            send_sem=a2a_send,
            recv_sem=a2a_recv,
            device_id=(other, lax.rem(me + r, OWNERS)),
            device_id_type=MESH,
        ).start()
        return carry

    lax.fori_loop(0, OWNERS, post, 0)

    def build(slots):
        base = (
            lax.broadcasted_iota(jnp.int32, (128, BLK), 0).astype(F32).astype(BF).reshape(8, 16, BLK)
        )
        for j in range(NB):
            cols = slice(j * BLK, (j + 1) * BLK)
            place = links_ref[:, cols] + lax.broadcasted_iota(jnp.int32, (8, BLK), 1) + HW
            weights = [
                jnp.broadcast_to(lw_ref[s : s + 1, cols], (16, BLK)).astype(BF)[None] for s in range(slots)
            ]

            def piece(k, carry):
                key = (place - k * 128).astype(F32)
                total = jnp.zeros((8, 16, BLK), BF)
                for s in range(slots):
                    spot = jnp.broadcast_to(key[s : s + 1], (16, BLK)).astype(BF)[None]
                    total = total + jnp.where(base == spot, weights[s], zero)
                mixm[j, pl.ds(pl.multiple_of(k * 128, 128), 128), :] = total.reshape(128, BLK)
                return carry

            lax.fori_loop(0, SPAN // 128, piece, 0)

    pl.when(comp == 0)(lambda: build(3))
    pl.when(comp == 1)(lambda: build(7))

    def settled(ext, j, vmat):
        cols = slice(j * BLK, (j + 1) * BLK)
        linked = dot(ext[:, j * BLK : j * BLK + SPAN], mixm[j])
        own = ext[:, HW + j * BLK : HW + (j + 1) * BLK]
        value = ab[0:1, cols] * own.astype(F32) + ab[1:2, cols] * linked
        if vmat is not None:
            value = value + ab[2:3, cols] * dot(vmat, own)
        return value

    for copy in deep1:
        copy.wait()

    @pl.when(comp == 0)
    def _():
        for j in range(NB):
            ext2[:, HW + j * BLK : HW + (j + 1) * BLK] = advance(settled(ext1, j, None).astype(BF), j)

    @pl.when(comp == 1)
    def _():
        for j in range(NB):
            ext2[:, HW + j * BLK : HW + (j + 1) * BLK] = settled(ext1, j, vert_ref[...]).astype(BF)

    deep2 = halo(ext2, 1)
    for copy in deep2:
        copy.start()

    whole = pltpu.make_async_remote_copy(
        src_ref=send, dst_ref=recv, send_sem=a2a_send, recv_sem=a2a_recv,
        device_id=(other, me), device_id_type=MESH,
    )
    whole.wait_recv()
    summed = jnp.sum(recv[...].astype(F32), axis=0)
    imps[...] = jnp.zeros_like(imps)
    for ch in range(CH):
        for hi in range(8):
            imps[ch : ch + 1, hi * 128 : (hi + 1) * 128] = summed[ch * 8 + hi : ch * 8 + hi + 1, :]
    imp_ref[...] = imps[0:CH, :]
    top = lax.broadcasted_iota(jnp.int32, (TAIL, BLK), 0)

    def forced(j):
        cols = slice(j * BLK, (j + 1) * BLK)
        base = dot(pick_ref[...], state_ref[:, cols])
        return (base + jnp.where(top < CH, 0.5, 0.0) * (imps[:, cols] - base)).astype(BF)

    @pl.when(comp == 0)
    def _():
        for j in range(NB):
            tail1[:, HW + j * BLK : HW + (j + 1) * BLK] = advance(forced(j), j)

    @pl.when(comp == 1)
    def _():
        for j in range(NB):
            tail1[:, HW + j * BLK : HW + (j + 1) * BLK] = forced(j)

    shallow1 = halo(tail1, 2)
    for copy in shallow1:
        copy.start()

    for copy in deep2:
        copy.wait()

    @pl.when(comp == 0)
    def _():
        for j in range(NB):
            out_ref[:, j * BLK : (j + 1) * BLK] = settled(ext2, j, None).astype(BF)

    @pl.when(comp == 1)
    def _():
        for j in range(NB):
            out_ref[:, j * BLK : (j + 1) * BLK] = settled(ext2, j, vert_ref[...]).astype(BF)

    for copy in shallow1:
        copy.wait()

    @pl.when(comp == 0)
    def _():
        for j in range(NB):
            tail2[:, HW + j * BLK : HW + (j + 1) * BLK] = advance(settled(tail1, j, None).astype(BF), j)

    @pl.when(comp == 1)
    def _():
        for j in range(NB):
            own = slice(HW + j * BLK, HW + (j + 1) * BLK)
            deep = dot(pick_ref[...], ext2[:, own])
            tail2[:, own] = jnp.where(top < 12, settled(tail1, j, tvert_ref[...]), deep).astype(BF)

    shallow2 = halo(tail2, 3)
    for copy in shallow2:
        copy.start()
    for copy in shallow2:
        copy.wait()

    def finish(vmat):
        for j in range(NB):
            cols = slice(j * BLK, (j + 1) * BLK)
            last = settled(tail2, j, vmat).astype(BF)
            for ch in range(CH):
                rows = slice(ch * LEV, ch * LEV + TAIL)
                spread = dot(place_ref[ch * TAIL : (ch + 1) * TAIL, :], last)
                out_ref[rows, cols] = jnp.where(top < 3, spread, out_ref[rows, cols].astype(F32)).astype(BF)

    pl.when(comp == 0)(lambda: finish(None))
    pl.when(comp == 1)(lambda: finish(tvert_ref[...]))
    whole.wait_send()


def shards(state, links, link_weight, point_mass, flow, ov_src, ov_owner, ov_row, ov_weight):
    vm = pl.BlockSpec(memory_space=pltpu.VMEM)
    wide = 2 * HW + ROWS
    new, imported = pl.pallas_call(
        body,
        out_shape=(
            jax.ShapeDtypeStruct((CH * LEV, ROWS), BF),
            jax.ShapeDtypeStruct((CH, ROWS), F32),
        ),
        in_specs=[vm] * 14,
        out_specs=(vm, vm),
        scratch_shapes=[
            pltpu.VMEM((CH * LEV, wide), BF),
            pltpu.VMEM((CH * LEV, wide), BF),
            pltpu.VMEM((TAIL, wide), BF),
            pltpu.VMEM((TAIL, wide), BF),
            pltpu.VMEM((NB, SPAN, BLK), BF),
            pltpu.VMEM((NB, BLK, BLK), BF),
            pltpu.VMEM((8, ROWS), F32),
            pltpu.VMEM((CH * 8, 128), F32),
            pltpu.VMEM((5, ENT // 128, 128), F32),
            pltpu.VMEM((OWNERS * 8, CH * 128), F32),
            pltpu.VMEM((OWNERS, CH * 8, 128), BF),
            pltpu.VMEM((OWNERS, CH * 8, 128), BF),
            pltpu.VMEM((TAIL, ROWS), F32),
            pltpu.SemaphoreType.DMA((4, 2)),
            pltpu.SemaphoreType.DMA((4, 2)),
            pltpu.SemaphoreType.DMA,
            pltpu.SemaphoreType.DMA,
        ],
        compiler_params=pltpu.CompilerParams(
            collective_id=0, has_side_effects=True, vmem_limit_bytes=48 * 1024 * 1024
        ),
        name="coupled",
    )(
        state.reshape(CH * LEV, ROWS),
        links,
        link_weight,
        point_mass.reshape(1, ROWS),
        flow,
        ov_src.reshape(ENT // 128, 128),
        ov_owner.reshape(ENT // 128, 128),
        ov_row.reshape(ENT // 128, 128),
        ov_weight.reshape(ENT // 128, 128),
        *constants(),
    )
    return new.reshape(CH, LEV, ROWS), imported


def solution(mesh):
    in_specs = (
        P(None, None, ("comp", "dom")),
        P(None, ("comp", "dom")),
        P(None, ("comp", "dom")),
        P(("comp", "dom")),
        P(None, ("comp", "dom")),
        P(("comp", "dom")),
        P(("comp", "dom"), None),
        P(("comp", "dom")),
        P(("comp", "dom")),
    )
    out_specs = (P(None, None, ("comp", "dom")), P(None, ("comp", "dom")))
    return jax.shard_map(shards, mesh=mesh, in_specs=in_specs, out_specs=out_specs, check_vma=False)
```

profile of v0, /device:TPU:0, one launch (start us, length us, event | category | flops | bytes accessed | tf_op | source)
XLA Modules:
  0.0 54.7 jit_solution(9281914185836477920)
XLA Ops:
  0.6 0.0 copy-start.9
  0.6 0.7 %copy-done.9 = bf16[64,16]{1,0:T(8,128)(2,1)S(1)} copy-done((bf16[64,16]{1,0:T(8,128)(2,1)S(1)}, bf16[64,16]{1,0:T(8,128)(2,1)}, u32[]{:S(2)}) %copy-start.9) | copy-done | bytes 2072
  1.4 0.0 copy-start
  1.4 1.0 %copy-done = bf16[4,64,1024]{2,1,0:T(8,128)(2,1)S(1)} copy-done((bf16[4,64,1024]{2,1,0:T(8,128)(2,1)S(1)}, bf16[4,64,1024]{2,1,0:T(8,128)(2,1)}, u32[]{:S(2)}) %copy-start) | copy-done | bytes 524312
  2.4 0.0 copy-start.1
  2.4 0.9 %copy-done.1 = bf16[2,256,256]{2,1,0:T(8,128)(2,1)S(1)} copy-done((bf16[2,256,256]{2,1,0:T(8,128)(2,1)S(1)}, bf16[2,256,256]{2,1,0:T(8,128)(2,1)}, u32[]{:S(2)}) %copy-start.1) | copy-done | bytes 262168
  3.3 0.0 copy-start.2
  3.3 0.9 %copy-done.2 = bf16[256,256]{1,0:T(8,128)(2,1)S(1)} copy-done((bf16[256,256]{1,0:T(8,128)(2,1)S(1)}, bf16[256,256]{1,0:T(8,128)(2,1)}, u32[]{:S(2)}) %copy-start.2) | copy-done | bytes 131096
  4.3 0.0 copy-start.3
  4.3 0.8 %copy-done.3 = s32[8,1024]{1,0:T(8,128)S(1)} copy-done((s32[8,1024]{1,0:T(8,128)S(1)}, s32[8,1024]{1,0:T(8,128)}, u32[]{:S(2)}) %copy-start.3) | copy-done | bytes 32792
  5.0 0.0 copy-start.4
  5.0 0.8 %copy-done.4 = f32[8,1024]{1,0:T(8,128)S(1)} copy-done((f32[8,1024]{1,0:T(8,128)S(1)}, f32[8,1024]{1,0:T(8,128)}, u32[]{:S(2)}) %copy-start.4) | copy-done | bytes 32792
  5.8 0.0 copy-start.5
  5.8 0.8 %copy-done.5 = s32[8192]{0:T(1024)S(1)} copy-done((s32[8192]{0:T(1024)S(1)}, s32[8192]{0:T(1024)}, u32[]{:S(2)}) %copy-start.5) | copy-done | bytes 32792
  6.5 0.8 %copy-done.6 = s32[8192,1]{0,1:T(1,128)S(1)} copy-done((s32[8192,1]{0,1:T(1,128)S(1)}, s32[8192,1]{0,1:T(1,128)}, u32[]{:S(2)}) %copy-start.6) | copy-done | bytes 32792
  7.3 0.8 %copy-done.7 = s32[8192]{0:T(1024)S(1)} copy-done((s32[8192]{0:T(1024)S(1)}, s32[8192]{0:T(1024)}, u32[]{:S(2)}) %copy-start.7) | copy-done | bytes 32792
  8.0 0.8 %copy-done.8 = f32[8192]{0:T(1024)S(1)} copy-done((f32[8192]{0:T(1024)S(1)}, f32[8192]{0:T(1024)}, u32[]{:S(2)}) %copy-start.8) | copy-done | bytes 32792
  8.8 0.7 %copy-done.10 = f32[2,1024]{1,0:T(2,128)S(1)} copy-done((f32[2,1024]{1,0:T(2,128)S(1)}, f32[2,1024]{1,0:T(2,128)}, u32[]{:S(2)}) %copy-start.10) | copy-done | bytes 8216
  9.5 0.7 %copy-done.11 = bf16[16,256]{1,0:T(8,128)(2,1)S(1)} copy-done((bf16[16,256]{1,0:T(8,128)(2,1)S(1)}, bf16[16,256]{1,0:T(8,128)(2,1)}, u32[]{:S(2)}) %copy-start.11) | copy-done | bytes 8216
  10.2 0.7 %copy-done.12 = f32[1024]{0:T(1024)S(1)} copy-done((f32[1024]{0:T(1024)S(1)}, f32[1024]{0:T(1024)}, u32[]{:S(2)}) %copy-start.12) | copy-done | bytes 4120
  10.9 0.7 %copy-done.13 = bf16[16,16]{1,0:T(8,128)(2,1)S(1)} copy-done((bf16[16,16]{1,0:T(8,128)(2,1)S(1)}, bf16[16,16]{1,0:T(8,128)(2,1)}, u32[]{:S(2)}) %copy-start.13) | copy-done | bytes 536
  11.6 41.7 %coupled.1 = (bf16[256,1024]{1,0:T(8,128)(2,1)S(1)}, f32[4,1024]{1,0:T(4,128)S(1)}) custom-call(bf16[256,1024]{1,0:T(8,128)(2,1)S(1)} %bitcast.7, s32[8,1024]{1,0:T(8,128)S(1)} %copy-done.3, f32[8,1024]{1,0:T(8,128)S(1)} %copy-done.4, f32[1,1024]{1,0:T(1,128)S(1)} %bitcast.13, f32[2,1024]{1,0:T(2,128)S(1)} %copy-done.10, s32[64,128]{1,0:T(8,128)S(1)} %bitcast.9, ...), custom_call_target="tpu_custom_call" | custom-call | tf_op jit(solution)/shard_map/coupled/pallas_call | solution.py:367
  53.3 0.8 %copy.18 = bf16[4,64,1024]{2,1,0:T(8,128)(2,1)} copy(bf16[4,64,1024]{2,1,0:T(8,128)(2,1)S(1)} %bitcast.8) | data formatting | bytes 1048576
  54.1 0.6 %copy.19 = f32[4,1024]{1,0:T(4,128)} copy(f32[4,1024]{1,0:T(4,128)S(1)} %get-tuple-element.9) | data formatting | bytes 32768
  (7 shorter events, 0.0 us)
Async XLA Ops:
  0.6 0.7 %copy-start.9 = (bf16[64,16]{1,0:T(8,128)(2,1)S(1)}, bf16[64,16]{1,0:T(8,128)(2,1)}, u32[]{:S(2)}) copy-start(bf16[64,16]{1,0:T(8,128)(2,1)} %constant.13.clone.place_ref) | copy-start | bytes 6148
  1.4 1.0 %copy-start = (bf16[4,64,1024]{2,1,0:T(8,128)(2,1)S(1)}, bf16[4,64,1024]{2,1,0:T(8,128)(2,1)}, u32[]{:S(2)}) copy-start(bf16[4,64,1024]{2,1,0:T(8,128)(2,1)} %param.14) | copy-start | bytes 1572868
  2.4 0.9 %copy-start.1 = (bf16[2,256,256]{2,1,0:T(8,128)(2,1)S(1)}, bf16[2,256,256]{2,1,0:T(8,128)(2,1)}, u32[]{:S(2)}) copy-start(bf16[2,256,256]{2,1,0:T(8,128)(2,1)} %constant.10.clone.kxy_ref) | copy-start | bytes 786436
  3.3 0.9 %copy-start.2 = (bf16[256,256]{1,0:T(8,128)(2,1)S(1)}, bf16[256,256]{1,0:T(8,128)(2,1)}, u32[]{:S(2)}) copy-start(bf16[256,256]{1,0:T(8,128)(2,1)} %constant.11.clone.vert_ref) | copy-start | bytes 393220
  4.3 0.8 %copy-start.3 = (s32[8,1024]{1,0:T(8,128)S(1)}, s32[8,1024]{1,0:T(8,128)}, u32[]{:S(2)}) copy-start(s32[8,1024]{1,0:T(8,128)} %links_ref.1) | copy-start | bytes 98308
  5.0 0.8 %copy-start.4 = (f32[8,1024]{1,0:T(8,128)S(1)}, f32[8,1024]{1,0:T(8,128)}, u32[]{:S(2)}) copy-start(f32[8,1024]{1,0:T(8,128)} %lw_ref.1) | copy-start | bytes 98308
  5.8 0.8 %copy-start.5 = (s32[8192]{0:T(1024)S(1)}, s32[8192]{0:T(1024)}, u32[]{:S(2)}) copy-start(s32[8192]{0:T(1024)} %param.19) | copy-start | bytes 98308
  6.5 0.8 %copy-start.6 = (s32[8192,1]{0,1:T(1,128)S(1)}, s32[8192,1]{0,1:T(1,128)}, u32[]{:S(2)}) copy-start(s32[8192,1]{0,1:T(1,128)} %param.20) | copy-start | bytes 98308
  7.3 0.8 %copy-start.7 = (s32[8192]{0:T(1024)S(1)}, s32[8192]{0:T(1024)}, u32[]{:S(2)}) copy-start(s32[8192]{0:T(1024)} %param.21) | copy-start | bytes 98308
  8.0 0.8 %copy-start.8 = (f32[8192]{0:T(1024)S(1)}, f32[8192]{0:T(1024)}, u32[]{:S(2)}) copy-start(f32[8192]{0:T(1024)} %param.22) | copy-start | bytes 98308
  8.8 0.7 %copy-start.10 = (f32[2,1024]{1,0:T(2,128)S(1)}, f32[2,1024]{1,0:T(2,128)}, u32[]{:S(2)}) copy-start(f32[2,1024]{1,0:T(2,128)} %flow_ref.1) | copy-start | bytes 24580
  9.5 0.7 %copy-start.11 = (bf16[16,256]{1,0:T(8,128)(2,1)S(1)}, bf16[16,256]{1,0:T(8,128)(2,1)}, u32[]{:S(2)}) copy-start(bf16[16,256]{1,0:T(8,128)(2,1)} %constant.12.clone.pick_ref) | copy-start | bytes 24580
  10.2 0.7 %copy-start.12 = (f32[1024]{0:T(1024)S(1)}, f32[1024]{0:T(1024)}, u32[]{:S(2)}) copy-start(f32[1024]{0:T(1024)} %param.17) | copy-start | bytes 12292
  10.9 0.7 %copy-start.13 = (bf16[16,16]{1,0:T(8,128)(2,1)S(1)}, bf16[16,16]{1,0:T(8,128)(2,1)}, u32[]{:S(2)}) copy-start(bf16[16,16]{1,0:T(8,128)(2,1)} %constant.14.clone.tvert_ref) | copy-start | bytes 1540
where the time goes:
time: 55.5 us; the launch traced here: 54.7 us
  Pallas kernels  41.7 us (75%)
  local copies, waits for them, and re-layouts  12.3 us (22%)
  between operations  0.66 us (1%)
    pallas_call x1, Pallas kernels, shards(): pl.pallas_call(body, out_shape=(jax.ShapeDtypeStruct((CH * LEV, ROWS), BF...  41.7 us
    unnamed x30, local copies, waits for them, and re-layouts  12.3 us

commit v1 on v0

v1 whole, which is shorter than its diff:
```python
import math

import jax
import jax.numpy as jnp
import numpy as np
from jax import lax
from jax.experimental import pallas as pl
from jax.experimental.pallas import tpu as pltpu
from jax.sharding import PartitionSpec as P

CH = 4
LEV = 64
ROWS = 1024
HW = 512
BLK = 256
NB = ROWS // BLK
SPAN = BLK + 2 * HW
OWNERS = 64
PLANE = 16
ENT = 8192
SLAB = 1024
TAIL = 16
MESH = pl.DeviceIdType.MESH
BF = jnp.bfloat16
F32 = jnp.float32


def derivative():
    nodes = np.array([-1.0, -1.0 / math.sqrt(5.0), 1.0 / math.sqrt(5.0), 1.0])
    weights = np.ones(4)
    for column in range(4):
        for middle in range(4):
            if middle != column:
                weights[column] = weights[column] / (nodes[column] - nodes[middle])
    table = np.zeros((4, 4))
    for target in range(4):
        for column in range(4):
            if column != target:
                table[target, column] = weights[column] / weights[target] / (nodes[target] - nodes[column])
        table[target, target] = -np.sum(table[target])
    return table


def element_table():
    d = derivative()
    along_x = np.kron(np.eye(4), d)
    along_y = np.kron(d, np.eye(4))
    return jnp.asarray(-0.04 * np.concatenate([np.tile(along_x.T, (1, 16)), np.tile(along_y.T, (1, 16))]), F32)


def index(shape, dim):
    return lax.broadcasted_iota(jnp.int32, shape, dim)


def ones_where(mask):
    return jnp.where(mask, 1.0, 0.0)


def vertical(rows):
    r, c = index((rows, rows), 0), index((rows, rows), 1)
    level = r & (LEV - 1)
    up = ones_where((c == r + 1) & (level < LEV - 1))
    down = ones_where((c == r - 1) & (level > 0))
    here = ones_where(c == r) * (ones_where(level < LEV - 1) + ones_where(level > 0))
    return (up + down - here).astype(BF)


def dot(a, b):
    return lax.dot_general(a, b, (((1,), (0,)), ((), ())), preferred_element_type=F32)


def dot_t(a, b):
    return lax.dot_general(a, b, (((1,), (1,)), ((), ())), preferred_element_type=F32)


def body(
    state_in, links_in, lw_in, mass_in, flow_in, src_in, owner_in, row_in, w_in, kxy_in,
    out_ref, imp_ref,
    links_ref, lw_ref, mass_ref, flow_ref, src_ref, owner_ref, row_ref, w_ref, kxy_ref,
    load_sem, vert_ref, meta, wind, ext1, ext2, mixm, badv, ab,
    table, keys, values_ref, send, recv, row_send, row_recv, before, after, sums, imps,
    halo_send, halo_recv, plane_send, plane_recv, line_send, line_recv, end_send, end_recv,
):
    comp = lax.axis_index("comp")
    me = lax.axis_index("dom")
    other = 1 - comp
    mz, my, mx = me // 16, lax.rem(me // 4, 4), lax.rem(me, 4)
    row = me - mx
    right = lax.rem(me + 1, OWNERS)
    left = lax.rem(me + OWNERS - 1, OWNERS)
    next_row = lax.rem(row + 4, OWNERS)
    previous_row = lax.rem(row + OWNERS - 4, OWNERS)

    def plane(q, sign):
        dz, dy = q // 4, lax.rem(q, 4)
        return lax.rem(mz + sign * dz + 4, 4) * 16 + lax.rem(my + sign * dy + 4, 4) * 4 + mx

    mid = slice(ROWS, 2 * ROWS)

    pairs = (
        (state_in, ext1.at[:, mid]), (src_in, src_ref), (row_in, row_ref), (owner_in, owner_ref), (w_in, w_ref),
        (flow_in, flow_ref), (mass_in, mass_ref), (lw_in, lw_ref), (links_in, links_ref), (kxy_in, kxy_ref),
    )
    loads = [pltpu.make_async_copy(a, b, load_sem.at[i]) for i, (a, b) in enumerate(pairs)]
    for copy in loads:
        copy.start()
    barrier = pltpu.get_barrier_semaphore()

    def greet(q, carry):
        pl.semaphore_signal(barrier, inc=1, device_id=(other, plane(q, -1)), device_id_type=MESH)
        return carry

    for side in (left, right):
        pl.semaphore_signal(barrier, inc=1, device_id=(comp, side), device_id_type=MESH)
    for k in range(1, 4):
        pl.semaphore_signal(barrier, inc=1, device_id=(comp, row + lax.rem(mx + k, 4)), device_id_type=MESH)

    @pl.when(mx == 0)
    def _():
        for k in range(4):
            pl.semaphore_signal(barrier, inc=1, device_id=(comp, previous_row + k), device_id_type=MESH)

    @pl.when(mx == 3)
    def _():
        for k in range(4):
            pl.semaphore_signal(barrier, inc=1, device_id=(comp, next_row + k), device_id_type=MESH)

    lax.fori_loop(0, PLANE, greet, 0)

    def halo(ext, width, number):
        own = ext.shape[1] - 2 * width
        copies = []
        for side, src, dst, k in (
            (right, slice(own, own + width), slice(0, width), 0),
            (left, slice(width, 2 * width), slice(own + width, own + 2 * width), 1),
        ):
            copies.append(
                pltpu.make_async_remote_copy(
                    src_ref=ext.at[:, src],
                    dst_ref=ext.at[:, dst],
                    send_sem=halo_send.at[number, k],
                    recv_sem=halo_recv.at[number, k],
                    device_id=(comp, side),
                    device_id_type=MESH,
                )
            )
        return copies

    for copy in loads:
        copy.wait()

    meta[0:8, HW : HW + ROWS] = links_ref[...].astype(F32)
    meta[8:16, HW : HW + ROWS] = lw_ref[...]
    wind[:, mid] = jnp.concatenate([flow_ref[...], jnp.zeros((6, ROWS), F32)], axis=0)
    meta[16:24, HW : HW + ROWS] = jnp.concatenate(
        [mass_ref[...], flow_ref[...], jnp.zeros((5, ROWS), F32)], axis=0
    )
    element = index((16, BLK), 1) >> 4

    def factors(blocks):
        for b in blocks:
            cols = slice(b * BLK, (b + 1) * BLK)
            total = jnp.sum(meta[8:16, cols], axis=0, keepdims=True)
            mass = meta[16:17, cols]

            @pl.when(comp == 0)
            def _():
                inv = 1.0 / (mass + total)
                ab[0:1, cols] = mass * inv
                ab[1:2, cols] = inv

            @pl.when(comp == 1)
            def _():
                half = 0.5 / mass
                ab[0:1, cols] = 1.0 - half * total
                ab[1:2, cols] = half
                ab[2:3, cols] = 0.25 * meta[17:18, cols] * meta[17:18, cols]

    def slopes(blocks):
        for g in blocks:
            cols = slice(g * BLK, (g + 1) * BLK)
            slope = kxy_ref[0:16, :] * wind[0:1, cols] + kxy_ref[16:32, :] * wind[1:2, cols]
            for p in range(BLK // 16):
                badv[g, p * 16 : p * 16 + 16, :] = jnp.where(element == p, slope, 0.0).astype(BF)

    def combine(blocks):
        for b in blocks:
            cols = slice(b * BLK, (b + 1) * BLK)
            for k in range(SPAN // BLK):
                rows = slice(k * BLK, (k + 1) * BLK)
                part = mixm[b, rows, :]
                value = part.astype(F32) + dot(badv[b + k], part)
                if k == 2:
                    value = value + ab[0:1, cols] * badv[b + 2].astype(F32)
                mixm[b, rows, :] = value.astype(BF)

    own_blocks = range(2, 2 + NB)

    pl.semaphore_wait(barrier, PLANE + 7)
    small_halo = halo(meta, HW, 0) + halo(wind, ROWS, 1)
    deep_halo = [
        pltpu.make_async_remote_copy(
            src_ref=state_in,
            dst_ref=ext1.at[:, dst],
            send_sem=halo_send.at[2, k],
            recv_sem=halo_recv.at[2, k],
            device_id=(comp, side),
            device_id_type=MESH,
        )
        for side, dst, k in ((right, slice(0, ROWS), 0), (left, slice(2 * ROWS, 3 * ROWS), 1))
    ]
    for copy in small_halo + deep_halo:
        copy.start()

    for ch in range(CH):
        line = ext1[ch * LEV : ch * LEV + 1, mid].astype(F32)
        for hi in range(8):
            table[ch * 8 + hi : ch * 8 + hi + 1, :] = line[:, hi * 128 : (hi + 1) * 128]
    source = src_ref[...]
    target = row_ref[...]
    owner = owner_ref[...]
    relative = (
        jnp.bitwise_and(lax.shift_right_logical(owner, 4) - mz + 4, 3) * 16
        + jnp.bitwise_and(lax.shift_right_logical(owner, 2) - my + 4, 3) * 4
        + jnp.bitwise_and(owner, 3)
    )
    first = relative * 8 + lax.shift_right_logical(target, 7)
    keys[0] = jnp.bitwise_and(source, 127).astype(F32)
    keys[1] = lax.shift_right_logical(source, 7).astype(F32)
    keys[2] = jnp.bitwise_and(target, 127).astype(F32)
    keys[3] = first.astype(F32)
    keys[4] = (first - 256).astype(F32)
    sub = index((8, 16, SLAB), 0) * 16 + index((8, 16, SLAB), 1)
    lanes = sub.astype(F32).astype(BF)
    upper = (sub + 128).astype(F32).astype(BF)
    high = index((8, SLAB), 0).astype(F32)
    exported = table[...].astype(BF)
    one, zero = jnp.asarray(1.0, BF), jnp.asarray(0.0, BF)
    chunks = SLAB // 128

    def row_of(which, i):
        return jnp.concatenate([keys[which, pl.ds(i * chunks + k, 1), :] for k in range(chunks)], axis=1)

    def wide(x):
        return jnp.broadcast_to(x, (16, SLAB)).astype(BF)[None]

    def spots(which, i):
        key = wide(row_of(which, i))
        return jnp.concatenate(
            [jnp.where(part == key, one, zero).reshape(128, SLAB) for part in (lanes, upper)], axis=0
        )

    def first_part(i, total):
        hot = jnp.where(lanes == wide(row_of(0, i)), one, zero).reshape(128, SLAB)
        found = dot(exported, hot)
        chosen = high == row_of(1, i)
        weight = jnp.concatenate([w_ref[pl.ds(i * chunks + k, 1), :] for k in range(chunks)], axis=1)
        low = lanes == wide(row_of(2, i))
        rows = []
        for ch in range(CH):
            value = jnp.sum(jnp.where(chosen, found[ch * 8 : ch * 8 + 8], 0.0), axis=0, keepdims=True) * weight
            rows.append(jnp.where(low, wide(value), zero).reshape(128, SLAB))
        values = jnp.concatenate(rows, axis=0)
        values_ref[i] = values
        return total + dot_t(spots(3, i), values)

    def second_part(i, total):
        return total + dot_t(spots(4, i), values_ref[i])

    half_owners = OWNERS // 2

    def pack(part, total):
        for pair in range(2):
            parts = [
                total[:, c * 128 : (c + 1) * 128].reshape(half_owners, 8, 128) for c in (2 * pair, 2 * pair + 1)
            ]
            send[part * half_owners : (part + 1) * half_owners, pair * 16 : pair * 16 + 16, :] = jnp.concatenate(
                parts, axis=1
            ).astype(BF)

    def post(part):
        def one_post(q, carry):
            pltpu.make_async_remote_copy(
                src_ref=send.at[pl.ds(q * 4, 4)],
                dst_ref=recv.at[pl.ds(q * 4, 4)],
                send_sem=plane_send.at[part],
                recv_sem=plane_recv.at[part],
                device_id=(other, plane(q, 1)),
                device_id_type=MESH,
            ).start()
            return carry

        lax.fori_loop(part * PLANE // 2, (part + 1) * PLANE // 2, one_post, 0)

    start = jnp.zeros((256, CH * 128), F32)
    pack(0, lax.fori_loop(0, ENT // SLAB, first_part, start, unroll=True))
    post(0)
    pack(1, lax.fori_loop(0, ENT // SLAB, second_part, start, unroll=True))
    post(1)

    base_iota = index((128, BLK), 0).astype(F32).astype(BF).reshape(8, 16, BLK)

    def build(slots, blocks):
        for b in blocks:
            cols = slice(b * BLK, (b + 1) * BLK)
            place = meta[0:8, cols] + (index((8, BLK), 1) + HW).astype(F32)
            weights = [
                jnp.broadcast_to(meta[8 + s : 9 + s, cols] * ab[1:2, cols], (16, BLK)).astype(BF)[None] for s in range(slots)
            ]

            def piece(k, carry):
                key = place - (k * 128).astype(F32)
                total = jnp.zeros((8, 16, BLK), BF)
                for s in range(slots):
                    spot = jnp.broadcast_to(key[s : s + 1], (16, BLK)).astype(BF)[None]
                    total = total + jnp.where(base_iota == spot, weights[s], zero)
                mixm[b, pl.ds(pl.multiple_of(k * 128, 128), 128), :] = total.reshape(128, BLK)
                return carry

            lax.fori_loop(0, SPAN // 128, piece, 0)

    vert_ref[...] = vertical(CH * LEV)
    factors(own_blocks)

    @pl.when(comp == 0)
    def _():
        slopes(range(NB, 2 * NB))
        build(3, own_blocks)

    pl.when(comp == 1)(lambda: build(7, own_blocks))
    for copy in small_halo:
        copy.wait()
    sides = (0, 1, 6, 7)
    factors(sides)

    @pl.when(comp == 0)
    def _():
        slopes((0, 1, 2, 3, 8, 9, 10, 11))
        build(3, sides)
        combine(range(2 * NB))

    pl.when(comp == 1)(lambda: build(7, sides))

    def settled(window, own, b, vmat):
        cols = slice(b * BLK, (b + 1) * BLK)
        value = ab[0:1, cols] * own.astype(F32) + dot(window, mixm[b])
        if vmat is not None:
            value = value + ab[2:3, cols] * dot(vmat, own)
        return value

    def first_step(ext, b, vmat):
        own = ext[:, HW + b * BLK : HW + (b + 1) * BLK]
        return settled(ext[:, b * BLK : b * BLK + SPAN], own, b, vmat)

    def second_step(ext, j, vmat):
        own = ext[:, HW + j * BLK : HW + (j + 1) * BLK]
        return settled(ext[:, j * BLK : j * BLK + SPAN], own, j + 2, vmat)

    def arrived(part):
        rows = slice(part * half_owners, (part + 1) * half_owners)
        return pltpu.make_async_remote_copy(
            src_ref=send.at[rows], dst_ref=recv.at[rows], send_sem=plane_send.at[part], recv_sem=plane_recv.at[part],
            device_id=(other, me), device_id_type=MESH,
        )

    total = jnp.zeros((4, CH * 8, 128), F32)
    for part in range(2):
        arrived(part).wait_recv()
        rows = slice(part * half_owners, (part + 1) * half_owners)
        total = total + jnp.sum(recv[rows].astype(F32).reshape(PLANE // 2, 4, CH * 8, 128), axis=0)
    row_send[...] = total.astype(BF)
    line = []
    for k in range(1, 4):
        line.append(
            pltpu.make_async_remote_copy(
                src_ref=row_send, dst_ref=row_recv.at[k - 1], send_sem=line_send.at[k - 1], recv_sem=line_recv.at[k - 1],
                device_id=(comp, row + lax.rem(mx + k, 4)), device_id_type=MESH,
            )
        )

    def end(which, slot, target, source, k):
        return pltpu.make_async_remote_copy(
            src_ref=row_send.at[source], dst_ref=which.at[slot], send_sem=end_send.at[k], recv_sem=end_recv.at[k, slot],
            device_id=(comp, target), device_id_type=MESH,
        )

    ends = [end(before, mx, next_row, 3, 0), end(after, mx, previous_row + 3, 0, 1)]
    for copy in ends + line:
        copy.start()

    for copy in deep_halo:
        copy.wait()
    for copy in line:
        copy.wait()
    total = row_send[...].astype(F32)
    for k in range(3):
        total = total + row_recv[k].astype(F32)
    sums[1:5] = total

    @pl.when(mx == 0)
    def _():
        for k in range(4):
            end(before, k, next_row, 3, 0).wait_recv()
        sums[0] = jnp.sum(before[...].astype(F32), axis=0)

    @pl.when(mx == 3)
    def _():
        for k in range(4):
            end(after, k, previous_row + 3, 0, 1).wait_recv()
        sums[5] = jnp.sum(after[...].astype(F32), axis=0)

    for side in range(3):
        block = sums[mx + side]
        for ch in range(CH):
            for hi in range(8):
                cols = slice(side * ROWS + hi * 128, side * ROWS + (hi + 1) * 128)
                imps[ch : ch + 1, cols] = block[ch * 8 + hi : ch * 8 + hi + 1, :]
    imp_ref[...] = imps[0:CH, mid]
    top = index((TAIL, BLK), 0)

    for g in range(3 * NB):
        cols = slice(g * BLK, (g + 1) * BLK)
        for ch in range(CH):
            rows = slice(ch * LEV, ch * LEV + TAIL)
            old = ext1[rows, cols].astype(F32)
            new = old + 0.5 * (imps[ch : ch + 1, cols] - old)
            ext1[rows, cols] = jnp.where(top == 0, new, old).astype(BF)

    def steps(vmat):
        for b in range(2 * NB):
            ext2[:, b * BLK : (b + 1) * BLK] = first_step(ext1, b, vmat).astype(BF)
        for j in range(NB):
            out_ref[:, j * BLK : (j + 1) * BLK] = second_step(ext2, j, vmat).astype(BF)

    pl.when(comp == 0)(lambda: steps(None))
    pl.when(comp == 1)(lambda: steps(vert_ref[...]))
    for copy in ends:
        copy.wait_send()
    arrived(0).wait_send()
    arrived(1).wait_send()


def shards(state, links, link_weight, point_mass, flow, ov_src, ov_owner, ov_row, ov_weight):
    hbm = pl.BlockSpec(memory_space=pl.ANY)
    vm = pl.BlockSpec(memory_space=pltpu.VMEM)
    operands = (
        state.reshape(CH * LEV, ROWS),
        links,
        link_weight,
        point_mass.reshape(1, ROWS),
        flow,
        ov_src.reshape(ENT // 128, 128),
        ov_owner.reshape(ENT // 128, 128),
        ov_row.reshape(ENT // 128, 128),
        ov_weight.reshape(ENT // 128, 128),
        element_table(),
    )
    new, imported = pl.pallas_call(
        body,
        out_shape=(
            jax.ShapeDtypeStruct((CH * LEV, ROWS), BF),
            jax.ShapeDtypeStruct((CH, ROWS), F32),
        ),
        in_specs=[hbm] * 10,
        out_specs=(vm, vm),
        scratch_shapes=[pltpu.VMEM(x.shape, x.dtype) for x in operands[1:]]
        + [
            pltpu.SemaphoreType.DMA((10,)),
            pltpu.VMEM((CH * LEV, CH * LEV), BF),
            pltpu.VMEM((24, 2 * ROWS), F32),
            pltpu.VMEM((8, 3 * ROWS), F32),
            pltpu.VMEM((CH * LEV, 3 * ROWS), BF),
            pltpu.VMEM((CH * LEV, 2 * ROWS), BF),
            pltpu.VMEM((2 * NB, SPAN, BLK), BF),
            pltpu.VMEM((3 * NB, BLK, BLK), BF),
            pltpu.VMEM((8, 2 * ROWS), F32),
            pltpu.VMEM((CH * 8, 128), F32),
            pltpu.VMEM((5, ENT // 128, 128), F32),
            pltpu.VMEM((ENT // SLAB, CH * 128, SLAB), BF),
            pltpu.VMEM((OWNERS, CH * 8, 128), BF),
            pltpu.VMEM((OWNERS, CH * 8, 128), BF),
            pltpu.VMEM((4, CH * 8, 128), BF),
            pltpu.VMEM((3, 4, CH * 8, 128), BF),
            pltpu.VMEM((4, CH * 8, 128), BF),
            pltpu.VMEM((4, CH * 8, 128), BF),
            pltpu.VMEM((6, CH * 8, 128), F32),
            pltpu.VMEM((8, 3 * ROWS), F32),
            pltpu.SemaphoreType.DMA((3, 2)),
            pltpu.SemaphoreType.DMA((3, 2)),
            pltpu.SemaphoreType.DMA((2,)),
            pltpu.SemaphoreType.DMA((2,)),
            pltpu.SemaphoreType.DMA((3,)),
            pltpu.SemaphoreType.DMA((3,)),
            pltpu.SemaphoreType.DMA((2,)),
            pltpu.SemaphoreType.DMA((2, 4)),
        ],
        compiler_params=pltpu.CompilerParams(
            collective_id=0, has_side_effects=True, vmem_limit_bytes=56 * 1024 * 1024
        ),
        name="coupled",
    )(*operands)
    return new.reshape(CH, LEV, ROWS), imported


def solution(mesh):
    in_specs = (
        P(None, None, ("comp", "dom")),
        P(None, ("comp", "dom")),
        P(None, ("comp", "dom")),
        P(("comp", "dom")),
        P(None, ("comp", "dom")),
        P(("comp", "dom")),
        P(("comp", "dom"), None),
        P(("comp", "dom")),
        P(("comp", "dom")),
    )
    out_specs = (P(None, None, ("comp", "dom")), P(None, ("comp", "dom")))
    return jax.shard_map(shards, mesh=mesh, in_specs=in_specs, out_specs=out_specs, check_vma=False)
```

time: 55.5 us -> 45.1 us (0.81)
  local copies, waits for them, and re-layouts: 12.3 us -> 2.48 us
    unnamed x30 -> x4, local copies, waits for them, and re-layouts: 12.3 us -> 2.48 us
where the time goes in v1:
time: 45.1 us; the launch traced here: 44.4 us
  Pallas kernels  41.2 us (91%)
  local copies, waits for them, and re-layouts  2.48 us (5%)
  between operations  0.65 us (1%)
    pallas_call x1, Pallas kernels, shards(): pl.pallas_call(body, out_shape=(jax.ShapeDtypeStruct((CH * LEV, ROWS), BF...  41.2 us
    unnamed x4, local copies, waits for them, and re-layouts  2.48 us

profile of v1, /device:TPU:0, one launch (start us, length us, event | category | flops | bytes accessed | tf_op | source)
XLA Modules:
  0.0 44.4 jit_solution(13455186100025193132)
XLA Ops:
  0.6 41.2 %coupled.1 = (bf16[256,1024]{1,0:T(8,128)(2,1)}, f32[4,1024]{1,0:T(4,128)}) custom-call(bf16[256,1024]{1,0:T(8,128)(2,1)} %bitcast.7, s32[8,1024]{1,0:T(8,128)} %links_in.1, f32[8,1024]{1,0:T(8,128)} %lw_in.1, f32[1,1024]{1,0:T(1,128)} %bitcast.13, f32[2,1024]{1,0:T(2,128)} %flow_in.1, s32[64,128]{1,0:T(8,128)} %bitcast.9, s32[64,128]{1,0:T(8,128)} %bitcast.10, ...), custom_call_target="tpu_custom_call" | custom-call | tf_op jit(solution)/shard_map/coupled/pallas_call | solution.py:458
  41.9 0.0 copy-start
  41.9 1.9 %copy.14 = bf16[4,64,1024]{2,1,0:T(8,128)(2,1)} copy(bf16[4,64,1024]{2,1,0:T(8,128)(2,1)} %bitcast.8) | data formatting | bytes 1048576
  43.8 0.0 copy-done
  43.8 0.6 %copy.15 = f32[4,1024]{1,0:T(4,128)} copy(f32[4,1024]{1,0:T(4,128)S(1)} %copy-done) | data formatting | bytes 32768
Async XLA Ops:
  41.9 1.9 %copy-start = (f32[4,1024]{1,0:T(4,128)S(1)}, f32[4,1024]{1,0:T(4,128)}, u32[]{:S(2)}) copy-start(f32[4,1024]{1,0:T(4,128)} %get-tuple-element.9) | copy-start | bytes 49156

commit v2 on v1

--- a/solution.py
+++ b/solution.py
@@ -78,8 +78,8 @@
     out_ref, imp_ref,
     links_ref, lw_ref, mass_ref, flow_ref, src_ref, owner_ref, row_ref, w_ref, kxy_ref,
     load_sem, vert_ref, meta, wind, ext1, ext2, mixm, badv, ab,
-    table, keys, values_ref, send, recv, row_send, row_recv, before, after, sums, imps,
-    halo_send, halo_recv, plane_send, plane_recv, line_send, line_recv, end_send, end_recv,
+    table, keys, values_ref, send, recv, row_send, row_recv, before, after, sums, imps, relay,
+    halo_send, halo_recv, deep_send, deep_recv, relay_recv, forward_send, plane_send, plane_recv, line_send, line_recv, end_send, end_recv,
 ):
     comp = lax.axis_index("comp")
     me = lax.axis_index("dom")
@@ -119,11 +119,13 @@
     def _():
         for k in range(4):
             pl.semaphore_signal(barrier, inc=1, device_id=(comp, previous_row + k), device_id_type=MESH)
+        pl.semaphore_signal(barrier, inc=1, device_id=(comp, next_row), device_id_type=MESH)
 
     @pl.when(mx == 3)
     def _():
         for k in range(4):
             pl.semaphore_signal(barrier, inc=1, device_id=(comp, next_row + k), device_id_type=MESH)
+        pl.semaphore_signal(barrier, inc=1, device_id=(comp, previous_row + 3), device_id_type=MESH)
 
     lax.fori_loop(0, PLANE, greet, 0)
 
@@ -196,21 +198,43 @@
 
     own_blocks = range(2, 2 + NB)
 
-    pl.semaphore_wait(barrier, PLANE + 7)
+    at_start, at_end = mx == 0, mx == 3
+    pl.semaphore_wait(barrier, jnp.where(at_start | at_end, PLANE + 8, PLANE + 7))
     small_halo = halo(meta, HW, 0) + halo(wind, ROWS, 1)
-    deep_halo = [
-        pltpu.make_async_remote_copy(
-            src_ref=state_in,
-            dst_ref=ext1.at[:, dst],
-            send_sem=halo_send.at[2, k],
-            recv_sem=halo_recv.at[2, k],
-            device_id=(comp, side),
-            device_id_type=MESH,
-        )
-        for side, dst, k in ((right, slice(0, ROWS), 0), (left, slice(2 * ROWS, 3 * ROWS), 1))
-    ]
-    for copy in small_halo + deep_halo:
+    half_rows = CH * LEV // 2
+    sides = ((right, slice(0, ROWS)), (left, slice(2 * ROWS, 3 * ROWS)))
+
+    def deep(half, k):
+        rows = slice(half * half_rows, (half + 1) * half_rows)
+        side, dst = sides[k]
+        return pltpu.make_async_remote_copy(
+            src_ref=state_in.at[rows], dst_ref=ext1.at[rows, dst],
+            send_sem=deep_send.at[half, k], recv_sem=deep_recv.at[half, k],
+            device_id=(comp, side), device_id_type=MESH,
+        )
+
+    def to_relay(k):
+        return pltpu.make_async_remote_copy(
+            src_ref=state_in.at[half_rows : 2 * half_rows], dst_ref=relay,
+            send_sem=deep_send.at[1, k], recv_sem=relay_recv.at[k],
+            device_id=(comp, next_row + 3 if k == 0 else previous_row), device_id_type=MESH,
+        )
+
+    def from_relay(k):
+        return pltpu.make_async_remote_copy(
+            src_ref=relay, dst_ref=ext1.at[half_rows : 2 * half_rows, sides[k][1]],
+            send_sem=forward_send, recv_sem=deep_recv.at[1, k],
+            device_id=(comp, row if k == 0 else row + 3), device_id_type=MESH,
+        )
+
+    for copy in small_halo:
         copy.start()
+    for k, edge in ((0, at_end), (1, at_start)):
+        pl.when(edge)(to_relay(k).start)
+    for k in range(2):
+        deep(0, k).start()
+    for k, edge in ((0, at_end), (1, at_start)):
+        pl.when(jnp.logical_not(edge))(deep(1, k).start)
 
     for ch in range(CH):
         line = ext1[ch * LEV : ch * LEV + 1, mid].astype(F32)
@@ -328,18 +352,25 @@
         build(3, own_blocks)
 
     pl.when(comp == 1)(lambda: build(7, own_blocks))
+    for k, edge in ((0, at_end), (1, at_start)):
+
+        @pl.when(edge)
+        def _():
+            to_relay(k).wait_recv()
+            from_relay(k).start()
+
     for copy in small_halo:
         copy.wait()
-    sides = (0, 1, 6, 7)
-    factors(sides)
+    outer = (0, 1, 6, 7)
+    factors(outer)
 
     @pl.when(comp == 0)
     def _():
         slopes((0, 1, 2, 3, 8, 9, 10, 11))
-        build(3, sides)
+        build(3, outer)
         combine(range(2 * NB))
 
-    pl.when(comp == 1)(lambda: build(7, sides))
+    pl.when(comp == 1)(lambda: build(7, outer))
 
     def settled(window, own, b, vmat):
         cols = slice(b * BLK, (b + 1) * BLK)
@@ -388,8 +419,9 @@
     for copy in ends + line:
         copy.start()
 
-    for copy in deep_halo:
-        copy.wait()
+    for half in range(2):
+        for k in range(2):
+            deep(half, k).wait()
     for copy in line:
         copy.wait()
     total = row_send[...].astype(F32)
@@ -434,6 +466,8 @@
 
     pl.when(comp == 0)(lambda: steps(None))
     pl.when(comp == 1)(lambda: steps(vert_ref[...]))
+    pl.when(at_end)(from_relay(0).wait_send)
+    pl.when(at_start)(from_relay(1).wait_send)
     for copy in ends:
         copy.wait_send()
     arrived(0).wait_send()
@@ -485,8 +519,13 @@
             pltpu.VMEM((4, CH * 8, 128), BF),
             pltpu.VMEM((6, CH * 8, 128), F32),
             pltpu.VMEM((8, 3 * ROWS), F32),
-            pltpu.SemaphoreType.DMA((3, 2)),
-            pltpu.SemaphoreType.DMA((3, 2)),
+            pltpu.VMEM((CH * LEV // 2, ROWS), BF),
+            pltpu.SemaphoreType.DMA((2, 2)),
+            pltpu.SemaphoreType.DMA((2, 2)),
+            pltpu.SemaphoreType.DMA((2, 2)),
+            pltpu.SemaphoreType.DMA((2, 2)),
+            pltpu.SemaphoreType.DMA((2,)),
+            pltpu.SemaphoreType.DMA,
             pltpu.SemaphoreType.DMA((2,)),
             pltpu.SemaphoreType.DMA((2,)),
             pltpu.SemaphoreType.DMA((3,)),

time: 45.1 us -> 39.2 us (0.87)
  Pallas kernels: 41.2 us -> 35.3 us
    pallas_call x1, Pallas kernels: 41.2 us -> 35.3 us  [shards(): pl.pallas_call(body, out_shape=(jax.ShapeDtypeStruct((CH * LEV, ROWS), BF...]
where the time goes in v2:
time: 39.2 us; the launch traced here: 38.5 us
  Pallas kernels  35.3 us (90%)
  local copies, waits for them, and re-layouts  2.48 us (6%)
  between operations  0.65 us (2%)
    pallas_call x1, Pallas kernels, shards(): pl.pallas_call(body, out_shape=(jax.ShapeDtypeStruct((CH * LEV, ROWS), BF...  35.3 us
    unnamed x4, local copies, waits for them, and re-layouts  2.48 us

profile of v2, /device:TPU:0, one launch (start us, length us, event | category | flops | bytes accessed | tf_op | source)
XLA Modules:
  0.0 38.5 jit_solution(10592437812130488248)
XLA Ops:
  0.6 35.3 %coupled.1 = (bf16[256,1024]{1,0:T(8,128)(2,1)}, f32[4,1024]{1,0:T(4,128)}) custom-call(bf16[256,1024]{1,0:T(8,128)(2,1)} %bitcast.7, s32[8,1024]{1,0:T(8,128)} %links_in.1, f32[8,1024]{1,0:T(8,128)} %lw_in.1, f32[1,1024]{1,0:T(1,128)} %bitcast.13, f32[2,1024]{1,0:T(2,128)} %flow_in.1, s32[64,128]{1,0:T(8,128)} %bitcast.9, s32[64,128]{1,0:T(8,128)} %bitcast.10, ...), custom_call_target="tpu_custom_call" | custom-call | tf_op jit(solution)/shard_map/coupled/pallas_call | solution.py:492
  36.0 0.0 copy-start
  36.0 1.9 %copy.14 = bf16[4,64,1024]{2,1,0:T(8,128)(2,1)} copy(bf16[4,64,1024]{2,1,0:T(8,128)(2,1)} %bitcast.8) | data formatting | bytes 1048576
  37.9 0.0 copy-done
  37.9 0.6 %copy.15 = f32[4,1024]{1,0:T(4,128)} copy(f32[4,1024]{1,0:T(4,128)S(1)} %copy-done) | data formatting | bytes 32768
Async XLA Ops:
  36.0 1.9 %copy-start = (f32[4,1024]{1,0:T(4,128)S(1)}, f32[4,1024]{1,0:T(4,128)}, u32[]{:S(2)}) copy-start(f32[4,1024]{1,0:T(4,128)} %get-tuple-element.9) | copy-start | bytes 49156

commit v3 on v2

--- a/solution.py
+++ b/solution.py
@@ -472,6 +472,11 @@
         copy.wait_send()
     arrived(0).wait_send()
     arrived(1).wait_send()
+
+
+def publish(new_in, imp_in, new_out, imp_out):
+    new_out[...] = new_in[...]
+    imp_out[...] = imp_in[...]
 
 
 def shards(state, links, link_weight, point_mass, flow, ov_src, ov_owner, ov_row, ov_weight):
@@ -538,6 +543,20 @@
         ),
         name="coupled",
     )(*operands)
+    cut = 1
+    parts = [pl.BlockSpec((CH * LEV // cut, ROWS), lambda i: (i, 0)), pl.BlockSpec((CH, ROWS), lambda i: (0, 0))]
+    new, imported = pl.pallas_call(
+        publish,
+        out_shape=(
+            jax.ShapeDtypeStruct((CH * LEV, ROWS), BF),
+            jax.ShapeDtypeStruct((CH, ROWS), F32),
+        ),
+        grid=(cut,),
+        in_specs=parts,
+        out_specs=parts,
+        compiler_params=pltpu.CompilerParams(vmem_limit_bytes=56 * 1024 * 1024),
+        name="publish",
+    )(new, imported)
     return new.reshape(CH, LEV, ROWS), imported
 
 

time: 39.2 us -> 38.6 us (0.985)
  local copies, waits for them, and re-layouts: 2.48 us -> 0 us
  Pallas kernels: 35.3 us -> 37.2 us
    unnamed x4 -> x0, local copies, waits for them, and re-layouts: 2.48 us -> none
    pallas_call x0 -> x1, Pallas kernels: none -> 1.87 us  [shards(): pl.pallas_call(publish, out_shape=(jax.ShapeDtypeStruct((CH * LEV, ROWS),...]
where the time goes in v3:
time: 38.6 us; the launch traced here: 37.9 us
  Pallas kernels  37.2 us (96%)
  between operations  0.64 us (2%)
    pallas_call x1, Pallas kernels, shards(): pl.pallas_call(body, out_shape=(jax.ShapeDtypeStruct((CH * LEV, ROWS), BF...  35.3 us
    pallas_call x1, Pallas kernels, shards(): pl.pallas_call(publish, out_shape=(jax.ShapeDtypeStruct((CH * LEV, ROWS),...  1.87 us

profile of v3, /device:TPU:0, one launch (start us, length us, event | category | flops | bytes accessed | tf_op | source)
XLA Modules:
  0.0 37.9 jit_solution(14276033709119922867)
XLA Ops:
  0.6 35.3 %coupled.1 = (bf16[256,1024]{1,0:T(8,128)(2,1)}, f32[4,1024]{1,0:T(4,128)}) custom-call(bf16[256,1024]{1,0:T(8,128)(2,1)} %bitcast.7, s32[8,1024]{1,0:T(8,128)} %links_in.1, f32[8,1024]{1,0:T(8,128)} %lw_in.1, f32[1,1024]{1,0:T(1,128)} %bitcast.12, f32[2,1024]{1,0:T(2,128)} %flow_in.1, s32[64,128]{1,0:T(8,128)} %bitcast.8, s32[64,128]{1,0:T(8,128)} %bitcast.9, ...), custom_call_target="tpu_custom_call" | custom-call | tf_op jit(solution)/shard_map/coupled/pallas_call | solution.py:497
  36.0 1.9 %publish.1 = (bf16[256,1024]{1,0:T(8,128)(2,1)}, f32[4,1024]{1,0:T(4,128)}) custom-call(bf16[256,1024]{1,0:T(8,128)(2,1)} %get-tuple-element.6.new_in, f32[4,1024]{1,0:T(4,128)} %get-tuple-element.7.imp_in), custom_call_target="tpu_custom_call" | custom-call | tf_op jit(solution)/shard_map/publish/pallas_call | solution.py:548
